TPU v7x, 512 devices: a whole 4x8x8 slice. The times are simulated.
512 devices in a mesh: ctx: 16 (over z, core), head: 8 (over y_hi, x), rep: 4 (over y_lo).
Axes of the slice: x: 4, y: 8 (y_hi: 2, y_lo: 4; y = y_hi * 4 + y_lo), z: 8, core: 2. Of those that a mesh axis runs over, the one named last changes fastest.
Arguments:
- queries: bfloat16 [20480, 8192], P(('rep', 'ctx'), 'head'), parts along dimension 0, may hold values from -40 to 40
- keys: bfloat16 [20480, 1024], P(('rep', 'ctx'), 'head'), parts along dimension 0, may hold values from -25 to 25
- values: bfloat16 [20480, 1024], P(('rep', 'ctx'), 'head'), parts along dimension 0, may hold values from -6 to 6
- block_order: int32 [128], P('rep'), parts along dimension 0, may hold values from 0 to 31, each once
Outputs:
- attended: bfloat16 [20480, 8192], P(('rep', 'ctx'), 'head'), parts along dimension 0
There are 4 independent parts, one for each index of `rep`. A program takes and returns all parts, laid end to end along the dimension named above; each array names one. Nothing has to cross between parts.
Inputs may be any that keep to these rules, and one draw needn't show every extreme that they name: A permutation: stored block b, rows b * 160 to (b + 1) * 160 - 1, holds the sequence's block block_order[b].
All inputs are finite; a program needn't handle non-finite values.
Results may differ from a plain program's by a relative error of at most 0.0044.
Values may be sent and summed in bfloat16 or wider, within the bound.
No kernel may reach another device: no remote copies, remote signals or barrier semaphores. Data moves between devices by JAX's collectives and lax.ppermute only.
A program may use at most 64 MiB of HBM per device.

v0:
```python
import math

import jax
import jax.numpy as jnp
from jax import lax
from jax.sharding import PartitionSpec as P

QUERY_HEADS = 64
KEY_VALUE_HEADS = 8
HEAD_SIZE = 128


NEGATIVE_LIMIT = -1e30


def shifted(block, axis, distance):
    devices = range(lax.axis_size(axis))
    route = [((i - distance) % len(devices), i) for i in devices]
    return lax.ppermute(block, axis, route)


def positions_of(block_table, owner_index, block_rows):
    starts = lax.dynamic_slice_in_dim(block_table, owner_index * 2, 2, 0)
    offsets = jnp.arange(block_rows, dtype=jnp.int32)
    return (starts[:, None] * block_rows + offsets[None, :]).reshape(-1)


def attend_block(query_rows, query_pos, key_rows, value_rows, key_pos):
    scaling = 1.0 / math.sqrt(query_rows.shape[-1])
    scores = (
        jnp.einsum("rkgd,tkd->rkgt", query_rows, key_rows, preferred_element_type=jnp.float32)
        * scaling
    )
    visible = (key_pos[None, :] <= query_pos[:, None])[:, None, None, :]
    scores = jnp.where(visible, scores, NEGATIVE_LIMIT)
    maxima = jnp.max(scores, axis=-1)
    weights = jnp.where(visible, jnp.exp(scores - maxima[..., None]), 0.0).astype(jnp.bfloat16)
    totals = jnp.sum(weights, axis=-1, dtype=jnp.float32)
    weighted = jnp.einsum("rkgt,tkd->rkgd", weights, value_rows, preferred_element_type=jnp.float32)
    return (maxima, totals, weighted)


def absorb(running, block_result):
    maxima = jnp.maximum(running[0], block_result[0])
    rescale = jnp.exp(running[0] - maxima)
    incoming = jnp.exp(block_result[0] - maxima)
    totals = running[1] * rescale + block_result[1] * incoming
    weighted = running[2] * rescale[..., None] + block_result[2] * incoming[..., None]
    return (maxima, totals, weighted)


def absorb_group(running, query_rows, query_pos, key_rows, value_rows, key_pos, block_rows):
    for key_start in range(0, key_rows.shape[0], block_rows):
        key_block = key_rows[key_start : key_start + block_rows]
        value_block = value_rows[key_start : key_start + block_rows]
        pos_block = key_pos[key_start : key_start + block_rows]
        block_result = attend_block(query_rows, query_pos, key_block, value_block, pos_block)
        running = absorb(running, block_result)
    return running


def per_device(queries, keys, values, block_order):
    row_count, feature_width = queries.shape
    block_rows = row_count // 2
    kv_heads = keys.shape[1] // HEAD_SIZE
    group_width = QUERY_HEADS // KEY_VALUE_HEADS
    devices = lax.axis_size("ctx")
    self_index = lax.axis_index("ctx")
    query_own = queries.reshape(row_count, kv_heads, group_width, HEAD_SIZE)
    key_own = keys.reshape(row_count, kv_heads, HEAD_SIZE)
    value_own = values.reshape(row_count, kv_heads, HEAD_SIZE)
    own_pos = positions_of(block_order, self_index, block_rows)
    initial_state = (
        jnp.full((row_count, kv_heads, group_width), NEGATIVE_LIMIT, jnp.float32),
        jnp.zeros((row_count, kv_heads, group_width), jnp.float32),
        jnp.zeros(query_own.shape, jnp.float32),
    )
    later_steps = jnp.arange(1, devices, dtype=jnp.int32)
    running = absorb_group(
        initial_state, query_own, own_pos, key_own, value_own, own_pos, block_rows
    )

    def travel(carried, offset):
        running, key_now, value_now = carried
        key_now, value_now = shifted((key_now, value_now), "ctx", 1)
        owner_index = (self_index - offset) % devices
        key_pos = positions_of(block_order, owner_index, block_rows)
        running = absorb_group(running, query_own, own_pos, key_now, value_now, key_pos, block_rows)
        return ((running, key_now, value_now), offset)

    (running, key_last, value_last), spent = lax.scan(
        travel, (running, key_own, value_own), later_steps
    )
    attended = running[2] / running[1][..., None]
    return attended.astype(jnp.bfloat16).reshape(row_count, feature_width)


def solution(mesh):
    placed = (
        P(("rep", "ctx"), "head"),
        P(("rep", "ctx"), "head"),
        P(("rep", "ctx"), "head"),
        P("rep"),
    )
    return jax.shard_map(
        per_device, mesh=mesh, in_specs=placed, out_specs=P(("rep", "ctx"), "head"), check_vma=False
    )
```

profile of v0, /device:TPU:1, one launch (start us, length us, event | category | flops | bytes accessed | tf_op | source)
XLA Modules:
  0.0 281.8 jit_solution(9396635262672553095)
XLA Ops:
  8.3 2.0 copy.29
  10.7 3.5 %fusion.33 = f32[1,128,320,8]{1,3,2,0:T(8,128)} fusion(bf16[320,8,160]{2,1,0:T(8,128)(2,1)} %copy.29, f32[320,8]{1,0:T(8,128)S(1)} %copy.31, f32[320,8]{1,0:T(8,128)S(1)} %copy.30, f32[320,8]{1,0:T(8,128)S(1)} %copy.28, bf16[320,128]{1,0:T(8,128)(2,1)} %copy.86), kind=kOutput, calls=%fused_computation.65 | convolution fusion | flops 105840640 | bytes 2693120 | tf_op jit(solution)/shard_map/rkgt,tkd->rkgd/dot_general | solution.py:39
  15.6 2.9 %fusion.30 = f32[320,1,8,128]{3,2,0,1:T(8,128)} fusion(f32[1,128,320,8]{1,3,2,0:T(8,128)} %fusion.33, bf16[320,8,160]{2,1,0:T(8,128)(2,1)S(1)} %copy.32, f32[320,8]{1,0:T(8,128)S(1)} %copy.33, bf16[320,128]{1,0:T(8,128)(2,1)} %copy.86), kind=kOutput, calls=%fused_computation.61 | convolution fusion | flops 105512960 | bytes 3491840 | tf_op jit(solution)/shard_map/rkgt,tkd->rkgd/dot_general | solution.py:39
  19.2 259.8 %while.21 = (s32[]{:T(128)}, f32[320,1,8]{0,2,1:T(8,128)S(1)}, f32[320,1,8]{0,2,1:T(8,128)S(1)}, f32[320,1,8,128]{3,2,0,1:T(8,128)}, bf16[320,1,128]{2,0,1:T(8,1...) while((s32[]{:T(128)}, f32[320,1,8]{0,2,1:T(8,128)S(1)}, ...), condition=%wide.region_9.10_spmd.clone, body=%wide.region_4.9_spmd.clone.sunk | while | flops 429722240 | bytes 31631896 | solution.py:91
  19.2 3.5 %collective-permute-start = (bf16[320,1,128]{2,0,1:T(8,128)(2,1)}, bf16[320,1,128]{2,0,1:T(8,128)(2,1)S(1)}, u32[]{:S(2)}, u32[]{:S(2)}) collective-permute-start(bf16[320,1,128]{2,0,1:T(8,128)(2,1)} %get-tuple-element.368), channel_id=1, source_target_pairs={{480,0},{0,32},{32,64},{64,96},{96,128},{128,160},{160,192},{192,2... | collective-permute-start | bytes 245768 | tf_op jit(solution)/shard_map/while/body/eval_jaxpr/ppermute | solution.py:19
  24.4 2.6 collective-permute-done
  30.8 1.9 copy.61
  34.9 4.0 %fusion.91 = f32[320,1,8,128]{3,2,0,1:T(8,128)} fusion(f32[320,1,8,128]{3,2,0,1:T(8,128)S(1)} %fusion.90, bf16[320,8,160]{2,1,0:T(8,128)(2,1)S(1)} %copy-done.2, f32[320,1,8,128]{3,2,0,1:T(8,128)} %get-tuple-element.367, f32[320,8]{1,0:T(8,128)S(1)} %copy.62, f32[320,8]{1,0:T(8,128)S(1)} %copy.63, f32[320,8]{1,0:T(8,128)S(1)} %copy.64, ...), kind=kOutput, calls=%fused_computation.16.clone.1 | convolution fusion | flops 106496000 | bytes 5775360 | tf_op jit(solution)/shard_map/while/body/eval_jaxpr/rkgt,tkd->rkgd/dot_general | solution.py:39
  40.7 3.6 %collective-permute-done = bf16[320,1,128]{2,0,1:T(8,128)(2,1)S(1)} collective-permute-done((bf16[320,1,128]{2,0,1:T(8,128)(2,1)}, bf16[320,1,128]{2,0,1:T(8,128)(2,1)S(1)}, u32[]{:S(2)}, u32[]{:S(2)}) %collective-permute-start) | collective-permute-done | bytes 81952 | tf_op jit(solution)/shard_map/while/body/eval_jaxpr/ppermute | solution.py:19
  48.1 1.9 copy.61
  52.2 4.0 %fusion.91 = f32[320,1,8,128]{3,2,0,1:T(8,128)} fusion(f32[320,1,8,128]{3,2,0,1:T(8,128)S(1)} %fusion.90, bf16[320,8,160]{2,1,0:T(8,128)(2,1)S(1)} %copy-done.2, f32[320,1,8,128]{3,2,0,1:T(8,128)} %get-tuple-element.367, f32[320,8]{1,0:T(8,128)S(1)} %copy.62, f32[320,8]{1,0:T(8,128)S(1)} %copy.63, f32[320,8]{1,0:T(8,128)S(1)} %copy.64, ...), kind=kOutput, calls=%fused_computation.16.clone.1 | convolution fusion | flops 106496000 | bytes 5775360 | tf_op jit(solution)/shard_map/while/body/eval_jaxpr/rkgt,tkd->rkgd/dot_general | solution.py:39
  58.0 3.4 %collective-permute-done = bf16[320,1,128]{2,0,1:T(8,128)(2,1)S(1)} collective-permute-done((bf16[320,1,128]{2,0,1:T(8,128)(2,1)}, bf16[320,1,128]{2,0,1:T(8,128)(2,1)S(1)}, u32[]{:S(2)}, u32[]{:S(2)}) %collective-permute-start) | collective-permute-done | bytes 81952 | tf_op jit(solution)/shard_map/while/body/eval_jaxpr/ppermute | solution.py:19
  65.2 1.9 copy.61
  69.3 4.0 %fusion.91 = f32[320,1,8,128]{3,2,0,1:T(8,128)} fusion(f32[320,1,8,128]{3,2,0,1:T(8,128)S(1)} %fusion.90, bf16[320,8,160]{2,1,0:T(8,128)(2,1)S(1)} %copy-done.2, f32[320,1,8,128]{3,2,0,1:T(8,128)} %get-tuple-element.367, f32[320,8]{1,0:T(8,128)S(1)} %copy.62, f32[320,8]{1,0:T(8,128)S(1)} %copy.63, f32[320,8]{1,0:T(8,128)S(1)} %copy.64, ...), kind=kOutput, calls=%fused_computation.16.clone.1 | convolution fusion | flops 106496000 | bytes 5775360 | tf_op jit(solution)/shard_map/while/body/eval_jaxpr/rkgt,tkd->rkgd/dot_general | solution.py:39
  75.2 3.4 %collective-permute-done = bf16[320,1,128]{2,0,1:T(8,128)(2,1)S(1)} collective-permute-done((bf16[320,1,128]{2,0,1:T(8,128)(2,1)}, bf16[320,1,128]{2,0,1:T(8,128)(2,1)S(1)}, u32[]{:S(2)}, u32[]{:S(2)}) %collective-permute-start) | collective-permute-done | bytes 81952 | tf_op jit(solution)/shard_map/while/body/eval_jaxpr/ppermute | solution.py:19
  82.3 1.9 copy.61
  86.5 4.0 %fusion.91 = f32[320,1,8,128]{3,2,0,1:T(8,128)} fusion(f32[320,1,8,128]{3,2,0,1:T(8,128)S(1)} %fusion.90, bf16[320,8,160]{2,1,0:T(8,128)(2,1)S(1)} %copy-done.2, f32[320,1,8,128]{3,2,0,1:T(8,128)} %get-tuple-element.367, f32[320,8]{1,0:T(8,128)S(1)} %copy.62, f32[320,8]{1,0:T(8,128)S(1)} %copy.63, f32[320,8]{1,0:T(8,128)S(1)} %copy.64, ...), kind=kOutput, calls=%fused_computation.16.clone.1 | convolution fusion | flops 106496000 | bytes 5775360 | tf_op jit(solution)/shard_map/while/body/eval_jaxpr/rkgt,tkd->rkgd/dot_general | solution.py:39
  92.3 3.4 %collective-permute-done = bf16[320,1,128]{2,0,1:T(8,128)(2,1)S(1)} collective-permute-done((bf16[320,1,128]{2,0,1:T(8,128)(2,1)}, bf16[320,1,128]{2,0,1:T(8,128)(2,1)S(1)}, u32[]{:S(2)}, u32[]{:S(2)}) %collective-permute-start) | collective-permute-done | bytes 81952 | tf_op jit(solution)/shard_map/while/body/eval_jaxpr/ppermute | solution.py:19
  99.5 1.9 copy.61
  103.6 4.0 %fusion.91 = f32[320,1,8,128]{3,2,0,1:T(8,128)} fusion(f32[320,1,8,128]{3,2,0,1:T(8,128)S(1)} %fusion.90, bf16[320,8,160]{2,1,0:T(8,128)(2,1)S(1)} %copy-done.2, f32[320,1,8,128]{3,2,0,1:T(8,128)} %get-tuple-element.367, f32[320,8]{1,0:T(8,128)S(1)} %copy.62, f32[320,8]{1,0:T(8,128)S(1)} %copy.63, f32[320,8]{1,0:T(8,128)S(1)} %copy.64, ...), kind=kOutput, calls=%fused_computation.16.clone.1 | convolution fusion | flops 106496000 | bytes 5775360 | tf_op jit(solution)/shard_map/while/body/eval_jaxpr/rkgt,tkd->rkgd/dot_general | solution.py:39
  109.4 3.4 %collective-permute-done = bf16[320,1,128]{2,0,1:T(8,128)(2,1)S(1)} collective-permute-done((bf16[320,1,128]{2,0,1:T(8,128)(2,1)}, bf16[320,1,128]{2,0,1:T(8,128)(2,1)S(1)}, u32[]{:S(2)}, u32[]{:S(2)}) %collective-permute-start) | collective-permute-done | bytes 81952 | tf_op jit(solution)/shard_map/while/body/eval_jaxpr/ppermute | solution.py:19
  116.6 1.9 copy.61
  120.7 4.0 %fusion.91 = f32[320,1,8,128]{3,2,0,1:T(8,128)} fusion(f32[320,1,8,128]{3,2,0,1:T(8,128)S(1)} %fusion.90, bf16[320,8,160]{2,1,0:T(8,128)(2,1)S(1)} %copy-done.2, f32[320,1,8,128]{3,2,0,1:T(8,128)} %get-tuple-element.367, f32[320,8]{1,0:T(8,128)S(1)} %copy.62, f32[320,8]{1,0:T(8,128)S(1)} %copy.63, f32[320,8]{1,0:T(8,128)S(1)} %copy.64, ...), kind=kOutput, calls=%fused_computation.16.clone.1 | convolution fusion | flops 106496000 | bytes 5775360 | tf_op jit(solution)/shard_map/while/body/eval_jaxpr/rkgt,tkd->rkgd/dot_general | solution.py:39
  126.6 3.4 %collective-permute-done = bf16[320,1,128]{2,0,1:T(8,128)(2,1)S(1)} collective-permute-done((bf16[320,1,128]{2,0,1:T(8,128)(2,1)}, bf16[320,1,128]{2,0,1:T(8,128)(2,1)S(1)}, u32[]{:S(2)}, u32[]{:S(2)}) %collective-permute-start) | collective-permute-done | bytes 81952 | tf_op jit(solution)/shard_map/while/body/eval_jaxpr/ppermute | solution.py:19
  133.7 1.9 copy.61
  137.9 4.0 %fusion.91 = f32[320,1,8,128]{3,2,0,1:T(8,128)} fusion(f32[320,1,8,128]{3,2,0,1:T(8,128)S(1)} %fusion.90, bf16[320,8,160]{2,1,0:T(8,128)(2,1)S(1)} %copy-done.2, f32[320,1,8,128]{3,2,0,1:T(8,128)} %get-tuple-element.367, f32[320,8]{1,0:T(8,128)S(1)} %copy.62, f32[320,8]{1,0:T(8,128)S(1)} %copy.63, f32[320,8]{1,0:T(8,128)S(1)} %copy.64, ...), kind=kOutput, calls=%fused_computation.16.clone.1 | convolution fusion | flops 106496000 | bytes 5775360 | tf_op jit(solution)/shard_map/while/body/eval_jaxpr/rkgt,tkd->rkgd/dot_general | solution.py:39
  143.7 3.4 %collective-permute-done = bf16[320,1,128]{2,0,1:T(8,128)(2,1)S(1)} collective-permute-done((bf16[320,1,128]{2,0,1:T(8,128)(2,1)}, bf16[320,1,128]{2,0,1:T(8,128)(2,1)S(1)}, u32[]{:S(2)}, u32[]{:S(2)}) %collective-permute-start) | collective-permute-done | bytes 81952 | tf_op jit(solution)/shard_map/while/body/eval_jaxpr/ppermute | solution.py:19
  150.9 1.9 copy.61
  155.0 4.0 %fusion.91 = f32[320,1,8,128]{3,2,0,1:T(8,128)} fusion(f32[320,1,8,128]{3,2,0,1:T(8,128)S(1)} %fusion.90, bf16[320,8,160]{2,1,0:T(8,128)(2,1)S(1)} %copy-done.2, f32[320,1,8,128]{3,2,0,1:T(8,128)} %get-tuple-element.367, f32[320,8]{1,0:T(8,128)S(1)} %copy.62, f32[320,8]{1,0:T(8,128)S(1)} %copy.63, f32[320,8]{1,0:T(8,128)S(1)} %copy.64, ...), kind=kOutput, calls=%fused_computation.16.clone.1 | convolution fusion | flops 106496000 | bytes 5775360 | tf_op jit(solution)/shard_map/while/body/eval_jaxpr/rkgt,tkd->rkgd/dot_general | solution.py:39
  160.8 3.4 %collective-permute-done = bf16[320,1,128]{2,0,1:T(8,128)(2,1)S(1)} collective-permute-done((bf16[320,1,128]{2,0,1:T(8,128)(2,1)}, bf16[320,1,128]{2,0,1:T(8,128)(2,1)S(1)}, u32[]{:S(2)}, u32[]{:S(2)}) %collective-permute-start) | collective-permute-done | bytes 81952 | tf_op jit(solution)/shard_map/while/body/eval_jaxpr/ppermute | solution.py:19
  168.0 1.9 copy.61
  172.1 4.0 %fusion.91 = f32[320,1,8,128]{3,2,0,1:T(8,128)} fusion(f32[320,1,8,128]{3,2,0,1:T(8,128)S(1)} %fusion.90, bf16[320,8,160]{2,1,0:T(8,128)(2,1)S(1)} %copy-done.2, f32[320,1,8,128]{3,2,0,1:T(8,128)} %get-tuple-element.367, f32[320,8]{1,0:T(8,128)S(1)} %copy.62, f32[320,8]{1,0:T(8,128)S(1)} %copy.63, f32[320,8]{1,0:T(8,128)S(1)} %copy.64, ...), kind=kOutput, calls=%fused_computation.16.clone.1 | convolution fusion | flops 106496000 | bytes 5775360 | tf_op jit(solution)/shard_map/while/body/eval_jaxpr/rkgt,tkd->rkgd/dot_general | solution.py:39
  178.0 3.4 %collective-permute-done = bf16[320,1,128]{2,0,1:T(8,128)(2,1)S(1)} collective-permute-done((bf16[320,1,128]{2,0,1:T(8,128)(2,1)}, bf16[320,1,128]{2,0,1:T(8,128)(2,1)S(1)}, u32[]{:S(2)}, u32[]{:S(2)}) %collective-permute-start) | collective-permute-done | bytes 81952 | tf_op jit(solution)/shard_map/while/body/eval_jaxpr/ppermute | solution.py:19
  189.3 4.0 %fusion.91 = f32[320,1,8,128]{3,2,0,1:T(8,128)} fusion(f32[320,1,8,128]{3,2,0,1:T(8,128)S(1)} %fusion.90, bf16[320,8,160]{2,1,0:T(8,128)(2,1)S(1)} %copy-done.2, f32[320,1,8,128]{3,2,0,1:T(8,128)} %get-tuple-element.367, f32[320,8]{1,0:T(8,128)S(1)} %copy.62, f32[320,8]{1,0:T(8,128)S(1)} %copy.63, f32[320,8]{1,0:T(8,128)S(1)} %copy.64, ...), kind=kOutput, calls=%fused_computation.16.clone.1 | convolution fusion | flops 106496000 | bytes 5775360 | tf_op jit(solution)/shard_map/while/body/eval_jaxpr/rkgt,tkd->rkgd/dot_general | solution.py:39
  195.1 3.4 %collective-permute-done = bf16[320,1,128]{2,0,1:T(8,128)(2,1)S(1)} collective-permute-done((bf16[320,1,128]{2,0,1:T(8,128)(2,1)}, bf16[320,1,128]{2,0,1:T(8,128)(2,1)S(1)}, u32[]{:S(2)}, u32[]{:S(2)}) %collective-permute-start) | collective-permute-done | bytes 81952 | tf_op jit(solution)/shard_map/while/body/eval_jaxpr/ppermute | solution.py:19
  206.4 4.0 %fusion.91 = f32[320,1,8,128]{3,2,0,1:T(8,128)} fusion(f32[320,1,8,128]{3,2,0,1:T(8,128)S(1)} %fusion.90, bf16[320,8,160]{2,1,0:T(8,128)(2,1)S(1)} %copy-done.2, f32[320,1,8,128]{3,2,0,1:T(8,128)} %get-tuple-element.367, f32[320,8]{1,0:T(8,128)S(1)} %copy.62, f32[320,8]{1,0:T(8,128)S(1)} %copy.63, f32[320,8]{1,0:T(8,128)S(1)} %copy.64, ...), kind=kOutput, calls=%fused_computation.16.clone.1 | convolution fusion | flops 106496000 | bytes 5775360 | tf_op jit(solution)/shard_map/while/body/eval_jaxpr/rkgt,tkd->rkgd/dot_general | solution.py:39
  212.3 3.4 %collective-permute-done = bf16[320,1,128]{2,0,1:T(8,128)(2,1)S(1)} collective-permute-done((bf16[320,1,128]{2,0,1:T(8,128)(2,1)}, bf16[320,1,128]{2,0,1:T(8,128)(2,1)S(1)}, u32[]{:S(2)}, u32[]{:S(2)}) %collective-permute-start) | collective-permute-done | bytes 81952 | tf_op jit(solution)/shard_map/while/body/eval_jaxpr/ppermute | solution.py:19
  219.4 1.9 copy.61
  223.6 4.0 %fusion.91 = f32[320,1,8,128]{3,2,0,1:T(8,128)} fusion(f32[320,1,8,128]{3,2,0,1:T(8,128)S(1)} %fusion.90, bf16[320,8,160]{2,1,0:T(8,128)(2,1)S(1)} %copy-done.2, f32[320,1,8,128]{3,2,0,1:T(8,128)} %get-tuple-element.367, f32[320,8]{1,0:T(8,128)S(1)} %copy.62, f32[320,8]{1,0:T(8,128)S(1)} %copy.63, f32[320,8]{1,0:T(8,128)S(1)} %copy.64, ...), kind=kOutput, calls=%fused_computation.16.clone.1 | convolution fusion | flops 106496000 | bytes 5775360 | tf_op jit(solution)/shard_map/while/body/eval_jaxpr/rkgt,tkd->rkgd/dot_general | solution.py:39
  229.4 3.4 %collective-permute-done = bf16[320,1,128]{2,0,1:T(8,128)(2,1)S(1)} collective-permute-done((bf16[320,1,128]{2,0,1:T(8,128)(2,1)}, bf16[320,1,128]{2,0,1:T(8,128)(2,1)S(1)}, u32[]{:S(2)}, u32[]{:S(2)}) %collective-permute-start) | collective-permute-done | bytes 81952 | tf_op jit(solution)/shard_map/while/body/eval_jaxpr/ppermute | solution.py:19
  236.6 1.9 copy.61
  240.7 4.0 %fusion.91 = f32[320,1,8,128]{3,2,0,1:T(8,128)} fusion(f32[320,1,8,128]{3,2,0,1:T(8,128)S(1)} %fusion.90, bf16[320,8,160]{2,1,0:T(8,128)(2,1)S(1)} %copy-done.2, f32[320,1,8,128]{3,2,0,1:T(8,128)} %get-tuple-element.367, f32[320,8]{1,0:T(8,128)S(1)} %copy.62, f32[320,8]{1,0:T(8,128)S(1)} %copy.63, f32[320,8]{1,0:T(8,128)S(1)} %copy.64, ...), kind=kOutput, calls=%fused_computation.16.clone.1 | convolution fusion | flops 106496000 | bytes 5775360 | tf_op jit(solution)/shard_map/while/body/eval_jaxpr/rkgt,tkd->rkgd/dot_general | solution.py:39
  246.5 3.4 %collective-permute-done = bf16[320,1,128]{2,0,1:T(8,128)(2,1)S(1)} collective-permute-done((bf16[320,1,128]{2,0,1:T(8,128)(2,1)}, bf16[320,1,128]{2,0,1:T(8,128)(2,1)S(1)}, u32[]{:S(2)}, u32[]{:S(2)}) %collective-permute-start) | collective-permute-done | bytes 81952 | tf_op jit(solution)/shard_map/while/body/eval_jaxpr/ppermute | solution.py:19
  253.7 1.9 copy.61
  257.8 4.0 %fusion.91 = f32[320,1,8,128]{3,2,0,1:T(8,128)} fusion(f32[320,1,8,128]{3,2,0,1:T(8,128)S(1)} %fusion.90, bf16[320,8,160]{2,1,0:T(8,128)(2,1)S(1)} %copy-done.2, f32[320,1,8,128]{3,2,0,1:T(8,128)} %get-tuple-element.367, f32[320,8]{1,0:T(8,128)S(1)} %copy.62, f32[320,8]{1,0:T(8,128)S(1)} %copy.63, f32[320,8]{1,0:T(8,128)S(1)} %copy.64, ...), kind=kOutput, calls=%fused_computation.16.clone.1 | convolution fusion | flops 106496000 | bytes 5775360 | tf_op jit(solution)/shard_map/while/body/eval_jaxpr/rkgt,tkd->rkgd/dot_general | solution.py:39
  263.7 3.4 %collective-permute-done = bf16[320,1,128]{2,0,1:T(8,128)(2,1)S(1)} collective-permute-done((bf16[320,1,128]{2,0,1:T(8,128)(2,1)}, bf16[320,1,128]{2,0,1:T(8,128)(2,1)S(1)}, u32[]{:S(2)}, u32[]{:S(2)}) %collective-permute-start) | collective-permute-done | bytes 81952 | tf_op jit(solution)/shard_map/while/body/eval_jaxpr/ppermute | solution.py:19
  270.8 1.9 copy.61
  275.0 4.0 %fusion.91 = f32[320,1,8,128]{3,2,0,1:T(8,128)} fusion(f32[320,1,8,128]{3,2,0,1:T(8,128)S(1)} %fusion.90, bf16[320,8,160]{2,1,0:T(8,128)(2,1)S(1)} %copy-done.2, f32[320,1,8,128]{3,2,0,1:T(8,128)} %get-tuple-element.367, f32[320,8]{1,0:T(8,128)S(1)} %copy.62, f32[320,8]{1,0:T(8,128)S(1)} %copy.63, f32[320,8]{1,0:T(8,128)S(1)} %copy.64, ...), kind=kOutput, calls=%fused_computation.16.clone.1 | convolution fusion | flops 106496000 | bytes 5775360 | tf_op jit(solution)/shard_map/while/body/eval_jaxpr/rkgt,tkd->rkgd/dot_general | solution.py:39
  (478 shorter events, 122.8 us)
Async XLA Ops:
  0.0 5.8 %copy-start.3 = (bf16[320,1024]{1,0:T(8,128)(2,1)S(1)}, bf16[320,1024]{1,0:T(8,128)(2,1)}, u32[]{:S(2)}) copy-start(bf16[320,1024]{1,0:T(8,128)(2,1)} %param.6) | copy-start | bytes 1966084
  19.2 8.9 %copy-start = (bf16[320,1,8,128]{3,0,2,1:T(8,128)(2,1)}, bf16[320,1,8,128]{3,0,2,1:T(8,128)(2,1)S(1)}, u32[]{:S(2)}) copy-start(bf16[320,1,8,128]{3,0,2,1:T(8,128)(2,1)S(1)} %get-tuple-element.390) | copy-start | bytes 1966084 | tf_op jit(solution)/shard_map/while
  19.2 7.9 %collective-permute-start = (bf16[320,1,128]{2,0,1:T(8,128)(2,1)}, bf16[320,1,128]{2,0,1:T(8,128)(2,1)S(1)}, u32[]{:S(2)}, u32[]{:S(2)}) collective-permute-start(bf16[320,1,128]{2,0,1:T(8,128)(2,1)} %get-tuple-element.368), channel_id=1, source_target_pairs={{480,0},{0,32},{32,64},{64,96},{96,128},{128,160},{160,192},{192,2... | collective-permute-start | bytes 245768 | tf_op jit(solution)/shard_map/while/body/eval_jaxpr/ppermute | solution.py:19
  22.6 11.1 %collective-permute-start.1 = (bf16[320,1,128]{2,0,1:T(8,128)(2,1)}, bf16[320,1,128]{2,0,1:T(8,128)(2,1)S(1)}, u32[]{:S(2)}, u32[]{:S(2)}) collective-permute-start(bf16[320,1,128]{2,0,1:T(8,128)(2,1)} %get-tuple-element.369), channel_id=1, source_target_pairs={{480,0},{0,32},{32,64},{64,96},{96,128},{128,160},{160,192},{192,2... | collective-permute-start | bytes 245768 | tf_op jit(solution)/shard_map/while/body/eval_jaxpr/ppermute | solution.py:19
  38.9 6.4 %copy-start = (bf16[320,1,8,128]{3,0,2,1:T(8,128)(2,1)}, bf16[320,1,8,128]{3,0,2,1:T(8,128)(2,1)S(1)}, u32[]{:S(2)}) copy-start(bf16[320,1,8,128]{3,0,2,1:T(8,128)(2,1)S(1)} %get-tuple-element.390) | copy-start | bytes 1966084 | tf_op jit(solution)/shard_map/while
  38.9 5.4 %collective-permute-start = (bf16[320,1,128]{2,0,1:T(8,128)(2,1)}, bf16[320,1,128]{2,0,1:T(8,128)(2,1)S(1)}, u32[]{:S(2)}, u32[]{:S(2)}) collective-permute-start(bf16[320,1,128]{2,0,1:T(8,128)(2,1)} %get-tuple-element.368), channel_id=1, source_target_pairs={{480,0},{0,32},{32,64},{64,96},{96,128},{128,160},{160,192},{192,2... | collective-permute-start | bytes 245768 | tf_op jit(solution)/shard_map/while/body/eval_jaxpr/ppermute | solution.py:19
  38.9 12.2 %collective-permute-start.1 = (bf16[320,1,128]{2,0,1:T(8,128)(2,1)}, bf16[320,1,128]{2,0,1:T(8,128)(2,1)S(1)}, u32[]{:S(2)}, u32[]{:S(2)}) collective-permute-start(bf16[320,1,128]{2,0,1:T(8,128)(2,1)} %get-tuple-element.369), channel_id=1, source_target_pairs={{480,0},{0,32},{32,64},{64,96},{96,128},{128,160},{160,192},{192,2... | collective-permute-start | bytes 245768 | tf_op jit(solution)/shard_map/while/body/eval_jaxpr/ppermute | solution.py:19
  56.2 6.3 %copy-start = (bf16[320,1,8,128]{3,0,2,1:T(8,128)(2,1)}, bf16[320,1,8,128]{3,0,2,1:T(8,128)(2,1)S(1)}, u32[]{:S(2)}) copy-start(bf16[320,1,8,128]{3,0,2,1:T(8,128)(2,1)S(1)} %get-tuple-element.390) | copy-start | bytes 1966084 | tf_op jit(solution)/shard_map/while
  56.2 5.3 %collective-permute-start = (bf16[320,1,128]{2,0,1:T(8,128)(2,1)}, bf16[320,1,128]{2,0,1:T(8,128)(2,1)S(1)}, u32[]{:S(2)}, u32[]{:S(2)}) collective-permute-start(bf16[320,1,128]{2,0,1:T(8,128)(2,1)} %get-tuple-element.368), channel_id=1, source_target_pairs={{480,0},{0,32},{32,64},{64,96},{96,128},{128,160},{160,192},{192,2... | collective-permute-start | bytes 245768 | tf_op jit(solution)/shard_map/while/body/eval_jaxpr/ppermute | solution.py:19
  56.2 12.0 %collective-permute-start.1 = (bf16[320,1,128]{2,0,1:T(8,128)(2,1)}, bf16[320,1,128]{2,0,1:T(8,128)(2,1)S(1)}, u32[]{:S(2)}, u32[]{:S(2)}) collective-permute-start(bf16[320,1,128]{2,0,1:T(8,128)(2,1)} %get-tuple-element.369), channel_id=1, source_target_pairs={{480,0},{0,32},{32,64},{64,96},{96,128},{128,160},{160,192},{192,2... | collective-permute-start | bytes 245768 | tf_op jit(solution)/shard_map/while/body/eval_jaxpr/ppermute | solution.py:19
  73.3 6.3 %copy-start = (bf16[320,1,8,128]{3,0,2,1:T(8,128)(2,1)}, bf16[320,1,8,128]{3,0,2,1:T(8,128)(2,1)S(1)}, u32[]{:S(2)}) copy-start(bf16[320,1,8,128]{3,0,2,1:T(8,128)(2,1)S(1)} %get-tuple-element.390) | copy-start | bytes 1966084 | tf_op jit(solution)/shard_map/while
  73.3 5.3 %collective-permute-start = (bf16[320,1,128]{2,0,1:T(8,128)(2,1)}, bf16[320,1,128]{2,0,1:T(8,128)(2,1)S(1)}, u32[]{:S(2)}, u32[]{:S(2)}) collective-permute-start(bf16[320,1,128]{2,0,1:T(8,128)(2,1)} %get-tuple-element.368), channel_id=1, source_target_pairs={{480,0},{0,32},{32,64},{64,96},{96,128},{128,160},{160,192},{192,2... | collective-permute-start | bytes 245768 | tf_op jit(solution)/shard_map/while/body/eval_jaxpr/ppermute | solution.py:19
  73.3 12.0 %collective-permute-start.1 = (bf16[320,1,128]{2,0,1:T(8,128)(2,1)}, bf16[320,1,128]{2,0,1:T(8,128)(2,1)S(1)}, u32[]{:S(2)}, u32[]{:S(2)}) collective-permute-start(bf16[320,1,128]{2,0,1:T(8,128)(2,1)} %get-tuple-element.369), channel_id=1, source_target_pairs={{480,0},{0,32},{32,64},{64,96},{96,128},{128,160},{160,192},{192,2... | collective-permute-start | bytes 245768 | tf_op jit(solution)/shard_map/while/body/eval_jaxpr/ppermute | solution.py:19
  90.4 6.3 %copy-start = (bf16[320,1,8,128]{3,0,2,1:T(8,128)(2,1)}, bf16[320,1,8,128]{3,0,2,1:T(8,128)(2,1)S(1)}, u32[]{:S(2)}) copy-start(bf16[320,1,8,128]{3,0,2,1:T(8,128)(2,1)S(1)} %get-tuple-element.390) | copy-start | bytes 1966084 | tf_op jit(solution)/shard_map/while
  90.4 5.3 %collective-permute-start = (bf16[320,1,128]{2,0,1:T(8,128)(2,1)}, bf16[320,1,128]{2,0,1:T(8,128)(2,1)S(1)}, u32[]{:S(2)}, u32[]{:S(2)}) collective-permute-start(bf16[320,1,128]{2,0,1:T(8,128)(2,1)} %get-tuple-element.368), channel_id=1, source_target_pairs={{480,0},{0,32},{32,64},{64,96},{96,128},{128,160},{160,192},{192,2... | collective-permute-start | bytes 245768 | tf_op jit(solution)/shard_map/while/body/eval_jaxpr/ppermute | solution.py:19
  90.4 12.0 %collective-permute-start.1 = (bf16[320,1,128]{2,0,1:T(8,128)(2,1)}, bf16[320,1,128]{2,0,1:T(8,128)(2,1)S(1)}, u32[]{:S(2)}, u32[]{:S(2)}) collective-permute-start(bf16[320,1,128]{2,0,1:T(8,128)(2,1)} %get-tuple-element.369), channel_id=1, source_target_pairs={{480,0},{0,32},{32,64},{64,96},{96,128},{128,160},{160,192},{192,2... | collective-permute-start | bytes 245768 | tf_op jit(solution)/shard_map/while/body/eval_jaxpr/ppermute | solution.py:19
  107.6 6.3 %copy-start = (bf16[320,1,8,128]{3,0,2,1:T(8,128)(2,1)}, bf16[320,1,8,128]{3,0,2,1:T(8,128)(2,1)S(1)}, u32[]{:S(2)}) copy-start(bf16[320,1,8,128]{3,0,2,1:T(8,128)(2,1)S(1)} %get-tuple-element.390) | copy-start | bytes 1966084 | tf_op jit(solution)/shard_map/while
  107.6 5.3 %collective-permute-start = (bf16[320,1,128]{2,0,1:T(8,128)(2,1)}, bf16[320,1,128]{2,0,1:T(8,128)(2,1)S(1)}, u32[]{:S(2)}, u32[]{:S(2)}) collective-permute-start(bf16[320,1,128]{2,0,1:T(8,128)(2,1)} %get-tuple-element.368), channel_id=1, source_target_pairs={{480,0},{0,32},{32,64},{64,96},{96,128},{128,160},{160,192},{192,2... | collective-permute-start | bytes 245768 | tf_op jit(solution)/shard_map/while/body/eval_jaxpr/ppermute | solution.py:19
  107.6 12.0 %collective-permute-start.1 = (bf16[320,1,128]{2,0,1:T(8,128)(2,1)}, bf16[320,1,128]{2,0,1:T(8,128)(2,1)S(1)}, u32[]{:S(2)}, u32[]{:S(2)}) collective-permute-start(bf16[320,1,128]{2,0,1:T(8,128)(2,1)} %get-tuple-element.369), channel_id=1, source_target_pairs={{480,0},{0,32},{32,64},{64,96},{96,128},{128,160},{160,192},{192,2... | collective-permute-start | bytes 245768 | tf_op jit(solution)/shard_map/while/body/eval_jaxpr/ppermute | solution.py:19
  124.7 6.3 %copy-start = (bf16[320,1,8,128]{3,0,2,1:T(8,128)(2,1)}, bf16[320,1,8,128]{3,0,2,1:T(8,128)(2,1)S(1)}, u32[]{:S(2)}) copy-start(bf16[320,1,8,128]{3,0,2,1:T(8,128)(2,1)S(1)} %get-tuple-element.390) | copy-start | bytes 1966084 | tf_op jit(solution)/shard_map/while
  124.7 5.3 %collective-permute-start = (bf16[320,1,128]{2,0,1:T(8,128)(2,1)}, bf16[320,1,128]{2,0,1:T(8,128)(2,1)S(1)}, u32[]{:S(2)}, u32[]{:S(2)}) collective-permute-start(bf16[320,1,128]{2,0,1:T(8,128)(2,1)} %get-tuple-element.368), channel_id=1, source_target_pairs={{480,0},{0,32},{32,64},{64,96},{96,128},{128,160},{160,192},{192,2... | collective-permute-start | bytes 245768 | tf_op jit(solution)/shard_map/while/body/eval_jaxpr/ppermute | solution.py:19
  124.7 12.0 %collective-permute-start.1 = (bf16[320,1,128]{2,0,1:T(8,128)(2,1)}, bf16[320,1,128]{2,0,1:T(8,128)(2,1)S(1)}, u32[]{:S(2)}, u32[]{:S(2)}) collective-permute-start(bf16[320,1,128]{2,0,1:T(8,128)(2,1)} %get-tuple-element.369), channel_id=1, source_target_pairs={{480,0},{0,32},{32,64},{64,96},{96,128},{128,160},{160,192},{192,2... | collective-permute-start | bytes 245768 | tf_op jit(solution)/shard_map/while/body/eval_jaxpr/ppermute | solution.py:19
  137.9 4.0 %copy-start.1 = (bf16[320,1,8,128]{3,0,2,1:T(8,128)(2,1)S(1)}, bf16[320,1,8,128]{3,0,2,1:T(8,128)(2,1)}, u32[]{:S(2)}) copy-start(bf16[320,1,8,128]{3,0,2,1:T(8,128)(2,1)} %copy-done) | copy-start | bytes 1966084 | tf_op jit(solution)/shard_map/while
  141.8 6.3 %copy-start = (bf16[320,1,8,128]{3,0,2,1:T(8,128)(2,1)}, bf16[320,1,8,128]{3,0,2,1:T(8,128)(2,1)S(1)}, u32[]{:S(2)}) copy-start(bf16[320,1,8,128]{3,0,2,1:T(8,128)(2,1)S(1)} %get-tuple-element.390) | copy-start | bytes 1966084 | tf_op jit(solution)/shard_map/while
  141.8 5.3 %collective-permute-start = (bf16[320,1,128]{2,0,1:T(8,128)(2,1)}, bf16[320,1,128]{2,0,1:T(8,128)(2,1)S(1)}, u32[]{:S(2)}, u32[]{:S(2)}) collective-permute-start(bf16[320,1,128]{2,0,1:T(8,128)(2,1)} %get-tuple-element.368), channel_id=1, source_target_pairs={{480,0},{0,32},{32,64},{64,96},{96,128},{128,160},{160,192},{192,2... | collective-permute-start | bytes 245768 | tf_op jit(solution)/shard_map/while/body/eval_jaxpr/ppermute | solution.py:19
  141.8 12.0 %collective-permute-start.1 = (bf16[320,1,128]{2,0,1:T(8,128)(2,1)}, bf16[320,1,128]{2,0,1:T(8,128)(2,1)S(1)}, u32[]{:S(2)}, u32[]{:S(2)}) collective-permute-start(bf16[320,1,128]{2,0,1:T(8,128)(2,1)} %get-tuple-element.369), channel_id=1, source_target_pairs={{480,0},{0,32},{32,64},{64,96},{96,128},{128,160},{160,192},{192,2... | collective-permute-start | bytes 245768 | tf_op jit(solution)/shard_map/while/body/eval_jaxpr/ppermute | solution.py:19
  155.0 4.0 %copy-start.1 = (bf16[320,1,8,128]{3,0,2,1:T(8,128)(2,1)S(1)}, bf16[320,1,8,128]{3,0,2,1:T(8,128)(2,1)}, u32[]{:S(2)}) copy-start(bf16[320,1,8,128]{3,0,2,1:T(8,128)(2,1)} %copy-done) | copy-start | bytes 1966084 | tf_op jit(solution)/shard_map/while
  159.0 6.3 %copy-start = (bf16[320,1,8,128]{3,0,2,1:T(8,128)(2,1)}, bf16[320,1,8,128]{3,0,2,1:T(8,128)(2,1)S(1)}, u32[]{:S(2)}) copy-start(bf16[320,1,8,128]{3,0,2,1:T(8,128)(2,1)S(1)} %get-tuple-element.390) | copy-start | bytes 1966084 | tf_op jit(solution)/shard_map/while
  159.0 5.3 %collective-permute-start = (bf16[320,1,128]{2,0,1:T(8,128)(2,1)}, bf16[320,1,128]{2,0,1:T(8,128)(2,1)S(1)}, u32[]{:S(2)}, u32[]{:S(2)}) collective-permute-start(bf16[320,1,128]{2,0,1:T(8,128)(2,1)} %get-tuple-element.368), channel_id=1, source_target_pairs={{480,0},{0,32},{32,64},{64,96},{96,128},{128,160},{160,192},{192,2... | collective-permute-start | bytes 245768 | tf_op jit(solution)/shard_map/while/body/eval_jaxpr/ppermute | solution.py:19
  159.0 12.0 %collective-permute-start.1 = (bf16[320,1,128]{2,0,1:T(8,128)(2,1)}, bf16[320,1,128]{2,0,1:T(8,128)(2,1)S(1)}, u32[]{:S(2)}, u32[]{:S(2)}) collective-permute-start(bf16[320,1,128]{2,0,1:T(8,128)(2,1)} %get-tuple-element.369), channel_id=1, source_target_pairs={{480,0},{0,32},{32,64},{64,96},{96,128},{128,160},{160,192},{192,2... | collective-permute-start | bytes 245768 | tf_op jit(solution)/shard_map/while/body/eval_jaxpr/ppermute | solution.py:19
  176.1 6.3 %copy-start = (bf16[320,1,8,128]{3,0,2,1:T(8,128)(2,1)}, bf16[320,1,8,128]{3,0,2,1:T(8,128)(2,1)S(1)}, u32[]{:S(2)}) copy-start(bf16[320,1,8,128]{3,0,2,1:T(8,128)(2,1)S(1)} %get-tuple-element.390) | copy-start | bytes 1966084 | tf_op jit(solution)/shard_map/while
  176.1 5.3 %collective-permute-start = (bf16[320,1,128]{2,0,1:T(8,128)(2,1)}, bf16[320,1,128]{2,0,1:T(8,128)(2,1)S(1)}, u32[]{:S(2)}, u32[]{:S(2)}) collective-permute-start(bf16[320,1,128]{2,0,1:T(8,128)(2,1)} %get-tuple-element.368), channel_id=1, source_target_pairs={{480,0},{0,32},{32,64},{64,96},{96,128},{128,160},{160,192},{192,2... | collective-permute-start | bytes 245768 | tf_op jit(solution)/shard_map/while/body/eval_jaxpr/ppermute | solution.py:19
  176.1 12.0 %collective-permute-start.1 = (bf16[320,1,128]{2,0,1:T(8,128)(2,1)}, bf16[320,1,128]{2,0,1:T(8,128)(2,1)S(1)}, u32[]{:S(2)}, u32[]{:S(2)}) collective-permute-start(bf16[320,1,128]{2,0,1:T(8,128)(2,1)} %get-tuple-element.369), channel_id=1, source_target_pairs={{480,0},{0,32},{32,64},{64,96},{96,128},{128,160},{160,192},{192,2... | collective-permute-start | bytes 245768 | tf_op jit(solution)/shard_map/while/body/eval_jaxpr/ppermute | solution.py:19
  193.2 6.3 %copy-start = (bf16[320,1,8,128]{3,0,2,1:T(8,128)(2,1)}, bf16[320,1,8,128]{3,0,2,1:T(8,128)(2,1)S(1)}, u32[]{:S(2)}) copy-start(bf16[320,1,8,128]{3,0,2,1:T(8,128)(2,1)S(1)} %get-tuple-element.390) | copy-start | bytes 1966084 | tf_op jit(solution)/shard_map/while
  193.2 5.3 %collective-permute-start = (bf16[320,1,128]{2,0,1:T(8,128)(2,1)}, bf16[320,1,128]{2,0,1:T(8,128)(2,1)S(1)}, u32[]{:S(2)}, u32[]{:S(2)}) collective-permute-start(bf16[320,1,128]{2,0,1:T(8,128)(2,1)} %get-tuple-element.368), channel_id=1, source_target_pairs={{480,0},{0,32},{32,64},{64,96},{96,128},{128,160},{160,192},{192,2... | collective-permute-start | bytes 245768 | tf_op jit(solution)/shard_map/while/body/eval_jaxpr/ppermute | solution.py:19
  193.3 12.0 %collective-permute-start.1 = (bf16[320,1,128]{2,0,1:T(8,128)(2,1)}, bf16[320,1,128]{2,0,1:T(8,128)(2,1)S(1)}, u32[]{:S(2)}, u32[]{:S(2)}) collective-permute-start(bf16[320,1,128]{2,0,1:T(8,128)(2,1)} %get-tuple-element.369), channel_id=1, source_target_pairs={{480,0},{0,32},{32,64},{64,96},{96,128},{128,160},{160,192},{192,2... | collective-permute-start | bytes 245768 | tf_op jit(solution)/shard_map/while/body/eval_jaxpr/ppermute | solution.py:19
  210.4 6.3 %copy-start = (bf16[320,1,8,128]{3,0,2,1:T(8,128)(2,1)}, bf16[320,1,8,128]{3,0,2,1:T(8,128)(2,1)S(1)}, u32[]{:S(2)}) copy-start(bf16[320,1,8,128]{3,0,2,1:T(8,128)(2,1)S(1)} %get-tuple-element.390) | copy-start | bytes 1966084 | tf_op jit(solution)/shard_map/while
  210.4 5.3 %collective-permute-start = (bf16[320,1,128]{2,0,1:T(8,128)(2,1)}, bf16[320,1,128]{2,0,1:T(8,128)(2,1)S(1)}, u32[]{:S(2)}, u32[]{:S(2)}) collective-permute-start(bf16[320,1,128]{2,0,1:T(8,128)(2,1)} %get-tuple-element.368), channel_id=1, source_target_pairs={{480,0},{0,32},{32,64},{64,96},{96,128},{128,160},{160,192},{192,2... | collective-permute-start | bytes 245768 | tf_op jit(solution)/shard_map/while/body/eval_jaxpr/ppermute | solution.py:19
  210.4 12.0 %collective-permute-start.1 = (bf16[320,1,128]{2,0,1:T(8,128)(2,1)}, bf16[320,1,128]{2,0,1:T(8,128)(2,1)S(1)}, u32[]{:S(2)}, u32[]{:S(2)}) collective-permute-start(bf16[320,1,128]{2,0,1:T(8,128)(2,1)} %get-tuple-element.369), channel_id=1, source_target_pairs={{480,0},{0,32},{32,64},{64,96},{96,128},{128,160},{160,192},{192,2... | collective-permute-start | bytes 245768 | tf_op jit(solution)/shard_map/while/body/eval_jaxpr/ppermute | solution.py:19
  227.5 6.3 %copy-start = (bf16[320,1,8,128]{3,0,2,1:T(8,128)(2,1)}, bf16[320,1,8,128]{3,0,2,1:T(8,128)(2,1)S(1)}, u32[]{:S(2)}) copy-start(bf16[320,1,8,128]{3,0,2,1:T(8,128)(2,1)S(1)} %get-tuple-element.390) | copy-start | bytes 1966084 | tf_op jit(solution)/shard_map/while
  227.5 5.3 %collective-permute-start = (bf16[320,1,128]{2,0,1:T(8,128)(2,1)}, bf16[320,1,128]{2,0,1:T(8,128)(2,1)S(1)}, u32[]{:S(2)}, u32[]{:S(2)}) collective-permute-start(bf16[320,1,128]{2,0,1:T(8,128)(2,1)} %get-tuple-element.368), channel_id=1, source_target_pairs={{480,0},{0,32},{32,64},{64,96},{96,128},{128,160},{160,192},{192,2... | collective-permute-start | bytes 245768 | tf_op jit(solution)/shard_map/while/body/eval_jaxpr/ppermute | solution.py:19
  227.5 12.0 %collective-permute-start.1 = (bf16[320,1,128]{2,0,1:T(8,128)(2,1)}, bf16[320,1,128]{2,0,1:T(8,128)(2,1)S(1)}, u32[]{:S(2)}, u32[]{:S(2)}) collective-permute-start(bf16[320,1,128]{2,0,1:T(8,128)(2,1)} %get-tuple-element.369), channel_id=1, source_target_pairs={{480,0},{0,32},{32,64},{64,96},{96,128},{128,160},{160,192},{192,2... | collective-permute-start | bytes 245768 | tf_op jit(solution)/shard_map/while/body/eval_jaxpr/ppermute | solution.py:19
  244.7 6.3 %copy-start = (bf16[320,1,8,128]{3,0,2,1:T(8,128)(2,1)}, bf16[320,1,8,128]{3,0,2,1:T(8,128)(2,1)S(1)}, u32[]{:S(2)}) copy-start(bf16[320,1,8,128]{3,0,2,1:T(8,128)(2,1)S(1)} %get-tuple-element.390) | copy-start | bytes 1966084 | tf_op jit(solution)/shard_map/while
  244.7 5.3 %collective-permute-start = (bf16[320,1,128]{2,0,1:T(8,128)(2,1)}, bf16[320,1,128]{2,0,1:T(8,128)(2,1)S(1)}, u32[]{:S(2)}, u32[]{:S(2)}) collective-permute-start(bf16[320,1,128]{2,0,1:T(8,128)(2,1)} %get-tuple-element.368), channel_id=1, source_target_pairs={{480,0},{0,32},{32,64},{64,96},{96,128},{128,160},{160,192},{192,2... | collective-permute-start | bytes 245768 | tf_op jit(solution)/shard_map/while/body/eval_jaxpr/ppermute | solution.py:19
  244.7 12.0 %collective-permute-start.1 = (bf16[320,1,128]{2,0,1:T(8,128)(2,1)}, bf16[320,1,128]{2,0,1:T(8,128)(2,1)S(1)}, u32[]{:S(2)}, u32[]{:S(2)}) collective-permute-start(bf16[320,1,128]{2,0,1:T(8,128)(2,1)} %get-tuple-element.369), channel_id=1, source_target_pairs={{480,0},{0,32},{32,64},{64,96},{96,128},{128,160},{160,192},{192,2... | collective-permute-start | bytes 245768 | tf_op jit(solution)/shard_map/while/body/eval_jaxpr/ppermute | solution.py:19
  261.8 6.3 %copy-start = (bf16[320,1,8,128]{3,0,2,1:T(8,128)(2,1)}, bf16[320,1,8,128]{3,0,2,1:T(8,128)(2,1)S(1)}, u32[]{:S(2)}) copy-start(bf16[320,1,8,128]{3,0,2,1:T(8,128)(2,1)S(1)} %get-tuple-element.390) | copy-start | bytes 1966084 | tf_op jit(solution)/shard_map/while
  261.8 5.3 %collective-permute-start = (bf16[320,1,128]{2,0,1:T(8,128)(2,1)}, bf16[320,1,128]{2,0,1:T(8,128)(2,1)S(1)}, u32[]{:S(2)}, u32[]{:S(2)}) collective-permute-start(bf16[320,1,128]{2,0,1:T(8,128)(2,1)} %get-tuple-element.368), channel_id=1, source_target_pairs={{480,0},{0,32},{32,64},{64,96},{96,128},{128,160},{160,192},{192,2... | collective-permute-start | bytes 245768 | tf_op jit(solution)/shard_map/while/body/eval_jaxpr/ppermute | solution.py:19
  261.8 12.0 %collective-permute-start.1 = (bf16[320,1,128]{2,0,1:T(8,128)(2,1)}, bf16[320,1,128]{2,0,1:T(8,128)(2,1)S(1)}, u32[]{:S(2)}, u32[]{:S(2)}) collective-permute-start(bf16[320,1,128]{2,0,1:T(8,128)(2,1)} %get-tuple-element.369), channel_id=1, source_target_pairs={{480,0},{0,32},{32,64},{64,96},{96,128},{128,160},{160,192},{192,2... | collective-permute-start | bytes 245768 | tf_op jit(solution)/shard_map/while/body/eval_jaxpr/ppermute | solution.py:19
  (29 other events, 84.9 us)
where the time goes:
time: 286 us; the launch traced here: 282 us
  local copies, waits for them, and re-layouts  96 us (34%)
  matrix products  91.3 us (32%)
  waiting for transfers between devices  50.6 us (18%)
  other arithmetic  28.3 us (10%)
  loops' own time  11.7 us (4%)
  starting transfers between devices  3.8 us (1%)
    dot_general x32, matrix products, attend_block(): jnp.einsum('rkgt,tkd->rkgd', weights, value_rows, preferred_element_type=...  73.3 us
    another operation x32, local copies, waits for them, and re-layouts  51.9 us
    ppermute x30, waiting for transfers between devices, shifted(): return lax.ppermute(block, axis, route)  50.6 us
    another operation x16, other arithmetic  19.6 us
    while x135, local copies, waits for them, and re-layouts  19.2 us
    dot_general x32, matrix products, attend_block(): jnp.einsum('rkgd,tkd->rkgt', query_rows, key_rows, preferred_element_type...  18 us
    another operation x1, loops' own time, per_device(): lax.scan(travel, (running, key_own, value_own), later_steps)  11.7 us
    dynamic_slice x15, local copies, waits for them, and re-layouts, per_device(): lax.scan(travel, (running, key_own, value_own), later_steps)  10.7 us
  transfers between devices with their start and end apart: 30, of which 15 were waited for; matrix products, arithmetic and copies ran while one was open for 42% of the time, Pallas kernels for 0%

commit v1 on v0

v1 whole, which is shorter than its diff:
```python
import functools
import math

import jax
import jax.numpy as jnp
from jax import lax
from jax.experimental import pallas as pl
from jax.experimental.pallas import tpu as pltpu
from jax.sharding import PartitionSpec as P

HEAD = 128
GROUP = 8
BLOCK = 160
ROWS = 2 * BLOCK
COLS = GROUP * BLOCK
CHIPS = 8
SUMROWS = HEAD + 16
SCALE = math.log2(math.e) / math.sqrt(HEAD)
NEG = -1e30
LIMIT = 2.0**100
TILES = ((0, 512), (512, 512), (1024, 256))


def dot_nt(a, b):
    return lax.dot_general(a, b, (((1,), (1,)), ((), ())), preferred_element_type=jnp.float32)


def dot_nn(a, b):
    return lax.dot_general(a, b, (((1,), (0,)), ((), ())), preferred_element_type=jnp.float32)


def stage(first, last, offsets, *refs):
    refs = list(refs)
    order_ref, me_ref = refs[:2]
    del refs[:2]
    if first:
        q_ref, own_ref, kv_ref = refs[:3]
        del refs[:3]
    else:
        qs_ref, m_in, acc_in, kv_ref = refs[:4]
        del refs[:4]
    if last:
        o_ref = refs.pop(0)
    elif first:
        qs_ref, m_out, acc_out = refs[:3]
        del refs[:3]
    else:
        m_out, acc_out = refs[:2]
        del refs[:2]
    vt = refs.pop(0)
    if last:
        acc_out, m_out = refs[:2]

    me = me_ref[0]
    z = me // 2
    span = kv_ref.shape[0]
    block_pos = []
    for off in offsets:
        dev = lax.rem(z + (off + CHIPS), CHIPS) * 2
        block_pos += [order_ref[dev * 2 + i] for i in range(4)]

    lane = lax.broadcasted_iota(jnp.int32, (1, span), 1)
    lane_pos = jnp.zeros((1, span), jnp.int32)
    for j, pos in enumerate(block_pos):
        lane_pos = jnp.where((lane >= j * BLOCK) & (lane < (j + 1) * BLOCK), pos, lane_pos)
    values_t = kv_ref[:, HEAD:].astype(jnp.float32).T

    if first:
        for a in range(2):
            key_rows = own_ref[a * BLOCK : (a + 1) * BLOCK, :]
            for h in range(GROUP):
                piece = q_ref[a * BLOCK : (a + 1) * BLOCK, h * HEAD : (h + 1) * HEAD]
                qs_ref[a * COLS + h * BLOCK : a * COLS + (h + 1) * BLOCK, :] = piece
                vt_rows = piece * key_rows
                m_out_rows = a * COLS + h * BLOCK
                refs[-1][m_out_rows : m_out_rows + BLOCK, :] = vt_rows
        for c in range(0, 2 * COLS, 256):
            diag = dot_nt(jnp.ones((8, HEAD), jnp.bfloat16), refs[-1][c : c + 256, :])
            m_out[:, c : c + 256] = diag[:1] * SCALE
        row = lax.broadcasted_iota(jnp.int32, (span, 1), 0)
        key_pos = jnp.zeros((span, 1), jnp.int32)
        for j, pos in enumerate(block_pos):
            key_pos = jnp.where((row >= j * BLOCK) & (row < (j + 1) * BLOCK), pos * BLOCK - j * BLOCK, key_pos)
        key_pos = key_pos + row
        vt[:HEAD, :] = values_t.astype(jnp.bfloat16)
        vt[HEAD:, :] = jnp.ones((SUMROWS - HEAD, span), jnp.bfloat16)

    def visible(a, col, width):
        pos = order_ref[me * 2 + a]
        if first:
            token = lax.rem(lax.broadcasted_iota(jnp.int32, (1, width), 1) + col, BLOCK)
            return key_pos <= token + pos * BLOCK
        return None

    stab = m_out if first else m_in
    over = jnp.zeros((1, 256), jnp.float32)
    for a in range(2):
        q_pos = order_ref[me * 2 + a]
        if not first:
            seen = lane_pos < q_pos
            vt[:HEAD, :] = jnp.where(seen, values_t, 0.0).astype(jnp.bfloat16)
            vt[HEAD:, :] = jnp.broadcast_to(jnp.where(seen, 1.0, 0.0), (SUMROWS - HEAD, span)).astype(jnp.bfloat16)
        for col, width in TILES:
            cols = slice(a * COLS + col, a * COLS + col + width)
            s = dot_nt(kv_ref[:, :HEAD], qs_ref[cols, :])
            p = jnp.exp2(s * SCALE - stab[:, cols])
            if first:
                p = jnp.where(visible(a, col, width), p, 0.0)
            new = dot_nn(vt[...], p.astype(jnp.bfloat16))
            if not first:
                new = new + acc_in[:, cols]
            acc_out[:, cols] = new
            if not first:
                m_out[:, cols] = m_in[:, cols]
            mass = jnp.where(new[HEAD : HEAD + 1] <= LIMIT, 0.0, 1.0)
            for i in range(0, width, 256):
                over = over + mass[:, i : i + 256]

    @pl.when(jnp.sum(over) > 0.0)
    def _():
        def tile(t, carry):
            a = t // (COLS // 256)
            col = (t - a * (COLS // 256)) * 256
            cols = pl.ds(pl.multiple_of(t * 256, 256), 256)
            q_pos = order_ref[me * 2 + a]
            token = lax.rem(lax.broadcasted_iota(jnp.int32, (1, 256), 1) + col, BLOCK) + q_pos * BLOCK
            acc_out[:, cols] = jnp.zeros((SUMROWS, 256), jnp.float32) if first else acc_in[:, cols]
            m_out[:, cols] = stab[:, cols]

            def block(j, carry):
                off = jnp.where(j < 4, offsets[0], offsets[-1])
                pos = order_ref[lax.rem(z + off + CHIPS, CHIPS) * 4 + lax.rem(j, 4)]
                rows = pl.ds(pl.multiple_of(j * BLOCK, BLOCK), BLOCK)
                s = dot_nt(kv_ref[rows, :HEAD], qs_ref[cols, :]) * SCALE
                key = lax.broadcasted_iota(jnp.int32, (BLOCK, 1), 0) + pos * BLOCK
                s = jnp.where(key <= token, s, NEG)
                m = m_out[:, cols]
                peak = jnp.maximum(m, jnp.max(s, axis=0, keepdims=True))
                p = jnp.exp2(s - peak).astype(jnp.bfloat16)
                value = jnp.concatenate(
                    [kv_ref[rows, HEAD:].astype(jnp.float32).T, jnp.ones((SUMROWS - HEAD, BLOCK), jnp.float32)], 0
                )
                acc_out[:, cols] = acc_out[:, cols] * jnp.exp2(m - peak) + dot_nn(value.astype(jnp.bfloat16), p)
                m_out[:, cols] = peak
                return carry

            return lax.fori_loop(0, span // BLOCK, block, carry)

        lax.fori_loop(0, 2 * COLS // 256, tile, 0)

    if last:
        for a in range(2):
            sums = acc_out[:, a * COLS : (a + 1) * COLS]
            full = (sums[:HEAD] * (1.0 / sums[HEAD : HEAD + 1])).T.astype(jnp.bfloat16)
            for h in range(GROUP):
                o_ref[a * BLOCK : (a + 1) * BLOCK, h * HEAD : (h + 1) * HEAD] = full[h * BLOCK : (h + 1) * BLOCK, :]


def run_stage(offsets, scalars, state, kv, last=False):
    first = len(state) == 2
    span = kv.shape[0]
    sums = jax.ShapeDtypeStruct((SUMROWS, 2 * COLS), jnp.float32)
    tops = jax.ShapeDtypeStruct((1, 2 * COLS), jnp.float32)
    rows = jax.ShapeDtypeStruct((2 * COLS, HEAD), jnp.bfloat16)
    scratch = [pltpu.VMEM((SUMROWS, span), jnp.bfloat16)]
    if last:
        out = jax.ShapeDtypeStruct((ROWS, GROUP * HEAD), jnp.bfloat16)
        scratch += [pltpu.VMEM(sums.shape, jnp.float32), pltpu.VMEM(tops.shape, jnp.float32)]
    elif first:
        out = (rows, tops, sums)
        scratch += [pltpu.VMEM(rows.shape, jnp.bfloat16)]
    else:
        out = (tops, sums)
    vmem = pl.BlockSpec(memory_space=pltpu.VMEM)
    smem = pl.BlockSpec(memory_space=pltpu.SMEM)
    pairs = span * 2 * COLS
    result = pl.pallas_call(
        functools.partial(stage, first, last, offsets),
        out_shape=out,
        in_specs=[smem, smem] + [vmem] * (len(state) + 1),
        out_specs=jax.tree.map(lambda _: vmem, out),
        scratch_shapes=scratch,
        compiler_params=pltpu.CompilerParams(vmem_limit_bytes=40 * 2**20),
        cost_estimate=pl.CostEstimate(
            flops=pairs * HEAD * 4, bytes_accessed=span * 512 + 4 * sums.size * 2, transcendentals=pairs
        ),
    )(*scalars, *state, kv)
    if last:
        return result
    if first:
        return list(result)
    return [state[0], *result]


def both_cores(block):
    pairs = [[2 * i, 2 * i + 1] for i in range(CHIPS)]
    return lax.all_gather(block, "ctx", tiled=True, axis_index_groups=pairs)


def away(block, hops):
    route = []
    for chip in range(CHIPS):
        route.append((chip * 2, (chip + hops) % CHIPS * 2))
        route.append((chip * 2 + 1, (chip - hops) % CHIPS * 2 + 1))
    return lax.ppermute(block, "ctx", route)


def per_device(queries, keys, values, block_order):
    me = lax.axis_index("ctx")
    scalars = (block_order, me.astype(jnp.int32).reshape(1))
    chip = both_cores(jnp.concatenate([keys, values], axis=1))
    one = away(chip, 1)
    two = away(chip, 2)
    state = run_stage((0,), scalars, [queries, keys], chip)
    three = away(one, 2)
    state = run_stage((-1, 1), scalars, state, both_cores(one))
    half = lax.dynamic_slice_in_dim(two, me % 2 * ROWS, ROWS, 0)
    four = away(half, 2)
    state = run_stage((-2, 2), scalars, state, both_cores(two))
    state = run_stage((-3, 3), scalars, state, both_cores(three))
    return run_stage((4,), scalars, state, both_cores(four), last=True)


def solution(mesh):
    placed = P(("rep", "ctx"), "head")
    return jax.shard_map(
        per_device,
        mesh=mesh,
        in_specs=(placed, placed, placed, P("rep")),
        out_specs=placed,
        check_vma=False,
    )
```

time: 286 us -> 96.3 us (0.34)
  the two profiles are of different devices: /device:TPU:1 before, /device:TPU:465 now
where the time goes in v1:
time: 96.3 us; the launch traced here: 95.9 us
  blocking collectives  48.4 us (50%)
  Pallas kernels  35.6 us (37%)
  starting transfers between devices  8.17 us (8%)
  local copies, waits for them, and re-layouts  2.64 us (3%)
    all_gather x5, blocking collectives, both_cores(): return lax.all_gather(block, 'ctx', tiled=True, axis_index_groups=pairs)  48.4 us
    pallas_call x5, Pallas kernels, run_stage(): pl.pallas_call(functools.partial(stage, first, last, offsets), out_shape=...  35.6 us
    ppermute x4, starting transfers between devices, away(): return lax.ppermute(block, 'ctx', route)  8.17 us
    unnamed x6, local copies, waits for them, and re-layouts  2.62 us
  transfers between devices with their start and end apart: 4, of which 0 were waited for; matrix products, arithmetic and copies ran while one was open for 0% of the time, Pallas kernels for 29%

profile of v1, /device:TPU:465, one launch (start us, length us, event | category | flops | bytes accessed | tf_op | source)
XLA Modules:
  0.0 95.9 jit_solution(9520631765219879899)
XLA Ops:
  0.0 0.9 pad_maximum_fusion
  0.9 2.4 %all_gather.15.refs_4_ = bf16[640,256]{1,0:T(8,128)(2,1)S(1)} all-gather(bf16[320,256]{1,0:T(8,128)(2,1)S(1)} %pad_maximum_fusion), channel_id=1, replica_groups={{0,32},{64,96},{128,160},{192,224},{256,288},{320,352},{384,416},{448,4..., dimensions={0}, use_global_device_ids=true | all-gather | bytes 491520 | tf_op jit(solution)/shard_map/all_gather | solution.py:197
  3.3 2.2 %collective-permute-start.1 = (bf16[640,256]{1,0:T(8,128)(2,1)S(1)}, bf16[640,256]{1,0:T(8,128)(2,1)S(1)}, u32[]{:S(2)}, u32[]{:S(2)}) collective-permute-start(bf16[640,256]{1,0:T(8,128)(2,1)S(1)} %all_gather.15.refs_4_), channel_id=1, source_target_pairs={{0,128},{32,416},{64,192},{96,480},{128,256},{160,32},{192,320},{2... | collective-permute-start | bytes 983048 | tf_op jit(solution)/shard_map/ppermute | solution.py:205
  5.5 2.2 %collective-permute-start = (bf16[640,256]{1,0:T(8,128)(2,1)S(1)}, bf16[640,256]{1,0:T(8,128)(2,1)S(1)}, u32[]{:S(2)}, u32[]{:S(2)}) collective-permute-start(bf16[640,256]{1,0:T(8,128)(2,1)S(1)} %all_gather.15.refs_4_), channel_id=1, source_target_pairs={{0,64},{32,480},{64,128},{96,32},{128,192},{160,96},{192,256},{224... | collective-permute-start | bytes 983048 | tf_op jit(solution)/shard_map/ppermute | solution.py:205
  7.7 0.0 copy-start
  7.7 0.9 copy-done
  8.6 0.0 copy-start.1
  8.6 0.7 copy-done.1
  9.2 0.0 copy-start.2
  9.2 1.1 %copy-done.2 = bf16[320,1024]{1,0:T(8,128)(2,1)S(1)} copy-done((bf16[320,1024]{1,0:T(8,128)(2,1)S(1)}, bf16[320,1024]{1,0:T(8,128)(2,1)}, u32[]{:S(2)}) %copy-start.2) | copy-done | bytes 655384
  10.3 19.0 %shard_map.46 = (bf16[2560,128]{1,0:T(8,128)(2,1)S(1)}, f32[1,2560]{1,0:T(1,128)S(1)}, f32[144,2560]{1,0:T(8,128)S(1)}) custom-call(s32[32]{0:T(128)S(1)} %copy-done.1, s32[1]{0:T(128)} %bitcast.refs_1_, bf16[320,1024]{1,0:T(8,128)(2,1)S(1)} %copy-done.2, bf16[320,128]{1,0:T(8,128)(2,1)S(1)} %copy-done, bf16[640,256]{1,0:T(8,128)(2,1)S(1)} %all_gather.15.refs_4_), custom_call_target="tpu_custom_call" | custom-call | flops 838860800 | bytes 3276800 | tf_op jit(solution)/shard_map/pallas_call | solution.py:177
  29.3 0.0 collective-permute-done.1
  29.3 1.9 %collective-permute-start.3 = (bf16[320,256]{1,0:T(8,128)(2,1)S(1)}, bf16[320,256]{1,0:T(8,128)(2,1)S(1)}, u32[]{:S(2)}, u32[]{:S(2)}) collective-permute-start(bf16[320,256]{1,0:T(8,128)(2,1)S(1)} %constant_dynamic-slice_fusion), channel_id=1, source_target_pairs={{0,128},{32,416},{64,192},{96,480},{128,256},{160,32},{192,320},{2... | collective-permute-start | bytes 491528 | tf_op jit(solution)/shard_map/ppermute | solution.py:205
  31.3 5.5 %all_gather.17.refs_5_ = bf16[1280,256]{1,0:T(8,128)(2,1)S(1)} all-gather(bf16[640,256]{1,0:T(8,128)(2,1)S(1)} %collective-permute-done.1), channel_id=1, replica_groups={{0,32},{64,96},{128,160},{192,224},{256,288},{320,352},{384,416},{448,4..., dimensions={0}, use_global_device_ids=true | all-gather | bytes 983040 | tf_op jit(solution)/shard_map/all_gather | solution.py:197
  36.8 0.0 collective-permute-done
  36.8 2.3 %all_gather.16.refs_5_ = bf16[1280,256]{1,0:T(8,128)(2,1)S(1)} all-gather(bf16[640,256]{1,0:T(8,128)(2,1)S(1)} %collective-permute-done), channel_id=1, replica_groups={{0,32},{64,96},{128,160},{192,224},{256,288},{320,352},{384,416},{448,4..., dimensions={0}, use_global_device_ids=true | all-gather | bytes 983040 | tf_op jit(solution)/shard_map/all_gather | solution.py:197
  39.0 1.9 %collective-permute-start.2 = (bf16[640,256]{1,0:T(8,128)(2,1)S(1)}, bf16[640,256]{1,0:T(8,128)(2,1)S(1)}, u32[]{:S(2)}, u32[]{:S(2)}) collective-permute-start(bf16[640,256]{1,0:T(8,128)(2,1)S(1)} %collective-permute-done), channel_id=1, source_target_pairs={{0,128},{32,416},{64,192},{96,480},{128,256},{160,32},{192,320},{2... | collective-permute-start | bytes 983048 | tf_op jit(solution)/shard_map/ppermute | solution.py:205
  40.9 4.2 %shard_map.47 = (f32[1,2560]{1,0:T(1,128)S(1)}, f32[144,2560]{1,0:T(8,128)S(1)}) custom-call(s32[32]{0:T(128)S(1)} %copy-done.1, s32[1]{0:T(128)} %bitcast.refs_1_, bf16[2560,128]{1,0:T(8,128)(2,1)S(1)} %get-tuple-element.14.refs_2_, f32[1,2560]{1,0:T(1,128)S(1)} %get-tuple-element.15.refs_3_, f32[144,2560]{1,0:T(8,128)S(1)} %get-tuple-element.16.refs_4_, ...), custom_call_target="tpu_custom_call" | custom-call | flops 1677721600 | bytes 3604480 | tf_op jit(solution)/shard_map/pallas_call | solution.py:177
  45.1 4.2 %shard_map.48 = (f32[1,2560]{1,0:T(1,128)S(1)}, f32[144,2560]{1,0:T(8,128)S(1)}) custom-call(s32[32]{0:T(128)S(1)} %copy-done.1, s32[1]{0:T(128)} %bitcast.refs_1_, bf16[2560,128]{1,0:T(8,128)(2,1)S(1)} %get-tuple-element.14.refs_2_, f32[1,2560]{1,0:T(1,128)S(1)} %get-tuple-element.17.refs_3_, f32[144,2560]{1,0:T(8,128)S(1)} %get-tuple-element.18.refs_4_, ...), custom_call_target="tpu_custom_call" | custom-call | flops 1677721600 | bytes 3604480 | tf_op jit(solution)/shard_map/pallas_call | solution.py:177
  49.3 0.0 collective-permute-done.3
  49.3 35.9 %all_gather.19.refs_5_ = bf16[640,256]{1,0:T(8,128)(2,1)S(1)} all-gather(bf16[320,256]{1,0:T(8,128)(2,1)S(1)} %collective-permute-done.3), channel_id=1, replica_groups={{0,32},{64,96},{128,160},{192,224},{256,288},{320,352},{384,416},{448,4..., dimensions={0}, use_global_device_ids=true | all-gather | bytes 491520 | tf_op jit(solution)/shard_map/all_gather | solution.py:197
  85.2 0.0 collective-permute-done.2
  85.2 2.4 %all_gather.18.refs_5_ = bf16[1280,256]{1,0:T(8,128)(2,1)S(1)} all-gather(bf16[640,256]{1,0:T(8,128)(2,1)S(1)} %collective-permute-done.2), channel_id=1, replica_groups={{0,32},{64,96},{128,160},{192,224},{256,288},{320,352},{384,416},{448,4..., dimensions={0}, use_global_device_ids=true | all-gather | bytes 983040 | tf_op jit(solution)/shard_map/all_gather | solution.py:197
  87.7 4.2 %shard_map.49 = (f32[1,2560]{1,0:T(1,128)S(1)}, f32[144,2560]{1,0:T(8,128)S(1)}) custom-call(s32[32]{0:T(128)S(1)} %copy-done.1, s32[1]{0:T(128)} %bitcast.refs_1_, bf16[2560,128]{1,0:T(8,128)(2,1)S(1)} %get-tuple-element.14.refs_2_, f32[1,2560]{1,0:T(1,128)S(1)} %get-tuple-element.19.refs_3_, f32[144,2560]{1,0:T(8,128)S(1)} %get-tuple-element.20.refs_4_, ...), custom_call_target="tpu_custom_call" | custom-call | flops 1677721600 | bytes 3604480 | tf_op jit(solution)/shard_map/pallas_call | solution.py:177
  91.8 4.1 %shard_map.50 = bf16[320,1024]{1,0:T(8,128)(2,1)} custom-call(s32[32]{0:T(128)S(1)} %copy-done.1, s32[1]{0:T(128)} %bitcast.refs_1_, bf16[2560,128]{1,0:T(8,128)(2,1)S(1)} %get-tuple-element.14.refs_2_, f32[1,2560]{1,0:T(1,128)S(1)} %get-tuple-element.21.refs_3_, f32[144,2560]{1,0:T(8,128)S(1)} %get-tuple-element.22.refs_4_, ...), custom_call_target="tpu_custom_call" | custom-call | flops 838860800 | bytes 3276800 | tf_op jit(solution)/shard_map/pallas_call | solution.py:177
  (1 shorter events, 0.0 us)
Async XLA Ops:
  3.3 26.0 %collective-permute-start.1 = (bf16[640,256]{1,0:T(8,128)(2,1)S(1)}, bf16[640,256]{1,0:T(8,128)(2,1)S(1)}, u32[]{:S(2)}, u32[]{:S(2)}) collective-permute-start(bf16[640,256]{1,0:T(8,128)(2,1)S(1)} %all_gather.15.refs_4_), channel_id=1, source_target_pairs={{0,128},{32,416},{64,192},{96,480},{128,256},{160,32},{192,320},{2... | collective-permute-start | bytes 983048 | tf_op jit(solution)/shard_map/ppermute | solution.py:205
  5.5 31.3 %collective-permute-start = (bf16[640,256]{1,0:T(8,128)(2,1)S(1)}, bf16[640,256]{1,0:T(8,128)(2,1)S(1)}, u32[]{:S(2)}, u32[]{:S(2)}) collective-permute-start(bf16[640,256]{1,0:T(8,128)(2,1)S(1)} %all_gather.15.refs_4_), channel_id=1, source_target_pairs={{0,64},{32,480},{64,128},{96,32},{128,192},{160,96},{192,256},{224... | collective-permute-start | bytes 983048 | tf_op jit(solution)/shard_map/ppermute | solution.py:205
  7.7 0.9 copy-start
  8.6 0.7 copy-start.1
  9.2 1.1 %copy-start.2 = (bf16[320,1024]{1,0:T(8,128)(2,1)S(1)}, bf16[320,1024]{1,0:T(8,128)(2,1)}, u32[]{:S(2)}) copy-start(bf16[320,1024]{1,0:T(8,128)(2,1)} %refs_2_.1) | copy-start | bytes 1966084
  29.3 20.0 %collective-permute-start.3 = (bf16[320,256]{1,0:T(8,128)(2,1)S(1)}, bf16[320,256]{1,0:T(8,128)(2,1)S(1)}, u32[]{:S(2)}, u32[]{:S(2)}) collective-permute-start(bf16[320,256]{1,0:T(8,128)(2,1)S(1)} %constant_dynamic-slice_fusion), channel_id=1, source_target_pairs={{0,128},{32,416},{64,192},{96,480},{128,256},{160,32},{192,320},{2... | collective-permute-start | bytes 491528 | tf_op jit(solution)/shard_map/ppermute | solution.py:205
  39.0 46.2 %collective-permute-start.2 = (bf16[640,256]{1,0:T(8,128)(2,1)S(1)}, bf16[640,256]{1,0:T(8,128)(2,1)S(1)}, u32[]{:S(2)}, u32[]{:S(2)}) collective-permute-start(bf16[640,256]{1,0:T(8,128)(2,1)S(1)} %collective-permute-done), channel_id=1, source_target_pairs={{0,128},{32,416},{64,192},{96,480},{128,256},{160,32},{192,320},{2... | collective-permute-start | bytes 983048 | tf_op jit(solution)/shard_map/ppermute | solution.py:205
